TPU v7x, 256 devices: a whole 4x4x8 slice. The times are simulated.
256 devices in a mesh: dp: 8 (over x, core), tensor: 32 (over y, z).
Axes of the slice: x: 4, y: 4, z: 8, core: 2. Of those that a mesh axis runs over, the one named last changes fastest.
Arguments:
- features: bfloat16 [6144, 8192], P('dp', 'tensor'), parts along dimension 0, may hold values from -6 to 6
- token_adapter_index: int32 [6144], P('dp'), parts along dimension 0, may hold values from 0 to 63, as said below
- projection_weight: bfloat16 [8192, 8192], P('tensor'), may hold values from -0.125 to 0.125
- shrink_weight: bfloat16 [8192, 4096], P('tensor'), may hold values from -0.0625 to 0.0625
- expand_weight: bfloat16 [4096, 8192], P(None, 'tensor'), may hold values from -0.75 to 0.75
Outputs:
- projected: float32 [6144, 8192], P('dp', 'tensor'), parts along dimension 0
There are 8 independent parts, one for each index of `dp`. A program takes and returns all parts, laid end to end along the dimension named above; an argument that names none is the same for every part. Nothing has to cross between parts.
Inputs may be any that keep to these rules, and one draw needn't show every extreme that they name: token_adapter_index never decreases along the tokens, so each adapter's tokens are contiguous; every adapter has 1 to 48 tokens, and one adapter has exactly 48.
All inputs are finite; a program needn't handle non-finite values.
Results may differ from a plain program's by a relative error of at most 0.0019.
Values may be sent and summed in bfloat16 or wider, within the bound.
A program may use at most 128 MiB of HBM per device.

v0:
```python
import jax
import jax.numpy as jnp
from jax import lax
from jax.sharding import PartitionSpec as P

ADAPTER_RANK = 64


def on_device(features, token_adapter_index, projection_weight, shrink_weight, expand_weight):
    rows = features.shape[0]
    rank_column_values = shrink_weight.shape[1]
    rank = ADAPTER_RANK
    adapters = rank_column_values // rank
    onehot = token_adapter_index[:, None] == jnp.arange(adapters, dtype=jnp.int32)[None, :]
    combined_output = jnp.dot(features, shrink_weight, preferred_element_type=jnp.float32).reshape(
        rows, adapters, rank
    )
    partial_shrink = jnp.sum(jnp.where(onehot[:, :, None], combined_output, 0.0), axis=1)
    shrink = lax.psum(partial_shrink, "tensor")
    shrunk = shrink.astype(jnp.bfloat16)
    widened_rank = (onehot.astype(jnp.bfloat16)[:, :, None] * shrunk[:, None, :]).reshape(
        rows, rank_column_values
    )
    lowrank_delta = jnp.dot(widened_rank, expand_weight, preferred_element_type=jnp.float32)
    base_partial_output = lax.psum_scatter(
        lax.dot_general(
            projection_weight,
            features,
            (((0,), (1,)), ((), ())),
            preferred_element_type=jnp.float32,
        ),
        "tensor",
        scatter_dimension=0,
        tiled=True,
    ).T
    return base_partial_output + lowrank_delta


def solution(mesh):
    in_specs = (P("dp", "tensor"), P("dp"), P("tensor", None), P("tensor", None), P(None, "tensor"))
    out_specs = P("dp", "tensor")
    return jax.shard_map(
        on_device, mesh=mesh, in_specs=in_specs, out_specs=out_specs, check_vma=False
    )
```

profile of v0, /device:TPU:4, one launch (start us, length us, event | category | flops | bytes accessed | tf_op | source)
XLA Modules:
  0.0 306.9 jit_solution(5828721270381377026)
XLA Ops:
  6.5 0.0 copy-start
  6.5 0.0 reduce-scatter.2.cloned.1.call-start
  6.5 14.3 %fusion.1 = f32[8192,768]{1,0:T(8,128)} fusion(bf16[256,8192]{1,0:T(8,128)(2,1)} %param.7, bf16[768,256]{1,0:T(8,128)(2,1)} %param.5), kind=kOutput, calls=%fused_computation.5 | convolution fusion | flops 3221225472 | bytes 29753344 | tf_op jit(solution)/shard_map/dot_general | solution.py:26
  20.8 0.0 copy-start.2
  20.8 0.0 copy-start.1
  20.9 0.0 reduce-scatter.2.cloned.1.call-update
  20.9 0.7 copy-done.2
  21.6 0.0 copy-done
  21.6 0.3 copy-done.1
  21.9 1.9 fusion.2
  23.7 2.3 select_reduce_fusion
  26.0 151.0 %all-reduce.1 = bf16[768,64]{0,1:T(8,128)(2,1)S(1)} all-reduce(f32[768,64]{0,1:T(8,128)S(1)} %select_reduce_fusion), channel_id=1, replica_groups=mesh['dp'=8,'tensor'=32] {'tensor'}, use_global_device_ids=true, to_apply=%region_2.3 | all-reduce | flops 49152 | bytes 294912 | tf_op jit(solution)/shard_map/psum | solution.py:19
  177.0 3.1 %broadcast_multiply_fusion = bf16[768,64,64]{0,2,1:T(8,128)(2,1)} fusion(bf16[768,64]{0,1:T(8,128)(2,1)S(1)} %all-reduce.1, bf16[768,64]{0,1:T(8,128)(2,1)S(1)} %get-tuple-element.5), kind=kLoop, calls=%fused_computation.1 | loop fusion | flops 3145728 | bytes 6488064 | tf_op jit(solution)/shard_map/mul | solution.py:21
  180.1 113.3 %reduce-scatter.2.cloned.1.call-done = f32[256,768]{1,0:T(8,128)} async-done(((f32[8192,768]{1,0:T(8,128)}), f32[256,768]{1,0:T(8,128)}) %reduce-scatter.2.cloned.1.call-update) | async-done | bytes 786448 | tf_op jit(solution)/shard_map/reduce_scatter | solution.py:25
  293.5 5.4 %convolution_add_fusion = f32[768,256]{0,1:T(8,128)S(1)} fusion(bf16[768,4096]{0,1:T(8,128)(2,1)} %bitcast.11, bf16[4096,256]{1,0:T(8,128)(2,1)} %param.9, f32[256,768]{1,0:T(8,128)} %reduce-scatter.2.cloned.1.call-done), kind=kOutput, calls=%fused_computation.2 | convolution fusion | flops 1610809344 | bytes 9961472 | tf_op jit(solution)/shard_map/dot_general | solution.py:24
  298.9 1.1 copy.10
  (1 shorter events, 0.0 us)
Async XLA Ops:
  6.5 15.0 %copy-start = (bf16[256,4096]{1,0:T(8,128)(2,1)S(1)}, bf16[256,4096]{1,0:T(8,128)(2,1)}, u32[]{:S(2)}) copy-start(bf16[256,4096]{1,0:T(8,128)(2,1)} %param.8) | copy-start | bytes 6291460
  6.5 286.9 %reduce-scatter.2.cloned.1.call-start = ((), (), s32[]{:S(2)}) async-start(), calls=%async_computation.1 | async-start | bytes 25952256 | tf_op jit(solution)/shard_map/reduce_scatter | solution.py:25
  20.8 0.7 copy-start.2
  20.8 1.0 copy-start.1
Sparse Core Ops, SparseCore 0:
  21.0 272.4 reduce-scatter.1
where the time goes:
time: 307 us
  blocking collectives  151 us (49%)
  waiting for transfers between devices  113 us (37%)
  matrix products  21.5 us (7%)
  between operations  13.4 us (4%)
  other arithmetic  5.42 us (2%)
    psum x1, blocking collectives, on_device(): shrink = lax.psum(partial_shrink, 'tensor')  151 us
    reduce_scatter x1, waiting for transfers between devices, on_device(): lax.psum_scatter(lax.dot_general(projection_weight, features, (((0,), (1,...  113 us
    dot_general x1, matrix products, on_device(): lax.dot_general(projection_weight, features, (((0,), (1,)), ((), ())), pr...  14.3 us
  transfers between devices with their start and end apart: 1, of which 1 were waited for; matrix products, arithmetic and copies ran while one was open for 2% of the time, Pallas kernels for 0%

commit v1 on v0

--- a/solution.py
+++ b/solution.py
@@ -1,9 +1,263 @@
 import jax
 import jax.numpy as jnp
 from jax import lax
+from jax.experimental import pallas as pl
+from jax.experimental.pallas import tpu as pltpu
 from jax.sharding import PartitionSpec as P
 
 ADAPTER_RANK = 64
+NX, NC, NY, NZ = 4, 2, 4, 8
+ROWS, KD, COLS = 768, 256, 256
+NB = 6
+BR = ROWS // NB
+HOPS = (3, 4)
+KORD = (0, 1, 7, 2, 6, 3, 5, 4)
+SLOT = {k: s for s, k in enumerate(KORD)}
+GROUPS = ((0, 1), (1, 2), (3, 2), (5, 2), (7, 1))
+HALF = KD // NC
+QUART = HALF // 2
+
+
+def base_kernel(
+    f_ref, w_ref, o_ref, fg, wg, ys, yr,
+    loc, wzs, wzr, wxs, wxr, wrs, wrr, wcs, wcr, fs, fr, yss, yrs,
+):
+    dp, tensor = lax.axis_index("dp"), lax.axis_index("tensor")
+    x, c = dp // NC, dp % NC
+    y, z = tensor // NZ, tensor % NZ
+
+    def at_z(k):
+        return {"tensor": y * NZ + (z + k) % NZ}
+
+    def at_y(d):
+        return {"tensor": ((y + d) % NY) * NZ + z}
+
+    def at_x(d):
+        return {"dp": ((x + d) % NX) * NC + c}
+
+    sibling = {"dp": x * NC + (1 - c)}
+
+    own_f = pltpu.make_async_copy(f_ref, fg.at[0], loc.at[0])
+    own_f.start()
+
+    def w_part(zz):
+        return w_ref.at[
+            pl.ds(pl.multiple_of(c * HALF, HALF), HALF),
+            pl.ds(pl.multiple_of((x * NZ + zz) * COLS, COLS), COLS),
+        ]
+
+    half = pl.ds(pl.multiple_of(c * HALF, HALF), HALF)
+    own_w = pltpu.make_async_copy(w_part(z), wg.at[x, 0, half], loc.at[1])
+    own_w.start()
+
+    peers = (
+        [at_z(k) for k in range(1, NZ)]
+        + [at_y(d) for d in range(1, NY)]
+        + [at_x(1), at_x(-1 + NX), sibling]
+    )
+    barrier = pltpu.get_barrier_semaphore()
+    for peer in peers:
+        pl.semaphore_signal(barrier, inc=1, device_id=peer, device_id_type=pl.DeviceIdType.MESH)
+    pl.semaphore_wait(barrier, len(peers))
+
+    def remote(src, dst, s, r, dev):
+        return pltpu.make_async_remote_copy(
+            src_ref=src, dst_ref=dst, send_sem=s, recv_sem=r,
+            device_id=dev, device_id_type=pl.DeviceIdType.MESH,
+        )
+
+    def wz(k):
+        return remote(
+            w_part((z + k) % NZ), wg.at[x, SLOT[k], half], wzs.at[k - 1], wzr.at[k - 1], at_z(k)
+        )
+
+    def wx(d, g, owner):
+        s0, n = GROUPS[g]
+        part = wg.at[owner, pl.ds(s0, n), half]
+        return remote(part, part, wxs.at[d, g], wxr.at[d, g], at_x(1 if d == 0 else NX - 1))
+
+    def wr(d, g, owner):
+        s0, n = GROUPS[g]
+        rows = pl.ds(pl.multiple_of(c * HALF + d * QUART, QUART), QUART)
+        part = wg.at[owner, pl.ds(s0, n), rows]
+        return remote(part, part, wrs.at[d, g], wrr.at[d, g], at_x(1 if d == 0 else NX - 1))
+
+    def wc(i, h, which):
+        owner = (x + (0, NX - 1, 1, 2)[i]) % NX
+        part = wg.at[owner, pl.ds(4 * h, 4), pl.ds(pl.multiple_of(which * HALF, HALF), HALF)]
+        return remote(part, part, wcs.at[i, h], wcr.at[i, h], sibling)
+
+    def fc(d, h, b):
+        src = SLOT[h] if d == 0 else SLOT[(NZ - h) % NZ]
+        dst = SLOT[h + 1] if d == 0 else SLOT[NZ - 1 - h]
+        rows = pl.ds(b * BR if isinstance(b, int) else pl.multiple_of(b * BR, BR), BR)
+        return remote(
+            fg.at[src, rows], fg.at[dst, rows], fs.at[d, h, b], fr.at[d, h, b],
+            at_z(1 if d == 0 else NZ - 1),
+        )
+
+    def yc(d, b):
+        rows = pl.ds(b * BR if isinstance(b, int) else pl.multiple_of(b * BR, BR), BR)
+        return remote(ys.at[d - 1, rows], yr.at[d - 1, rows], yss.at[d - 1, b], yrs.at[d - 1, b], at_y(d))
+
+    for k in KORD[1:]:
+        wz(k).start()
+    own_w.wait()
+    wx(0, 0, x).start()
+    wx(1, 0, x).start()
+    own_f.wait()
+    fc(0, 0, 0).start()
+    fc(1, 0, 0).start()
+    for g in range(1, len(GROUPS)):
+        s0, n = GROUPS[g]
+        for s in range(s0, s0 + n):
+            wz(KORD[s]).wait_recv()
+        wx(0, g, x).start()
+        wx(1, g, x).start()
+        if g == 2:
+            wc(0, 0, c).start()
+    wc(0, 1, c).start()
+
+    left, right = (x + NX - 1) % NX, (x + 1) % NX
+
+    def from_x(g):
+        wx(0, g, left).wait_recv()
+        wr(0, g, left).start()
+        wx(1, g, right).wait_recv()
+        wr(1, g, right).start()
+
+    def from_relay(g):
+        wr(0, g, (x + 2) % NX).wait_recv()
+        wr(1, g, (x + 2) % NX).wait_recv()
+
+    def forward(t, static):
+        def when(cond, fn):
+            if static:
+                if cond:
+                    fn()
+            else:
+                pl.when(cond)(fn)
+
+        def own():
+            fc(0, 0, t).start()
+            fc(1, 0, t).start()
+
+        when(t < NB, own)
+        for h in range(max(HOPS), 0, -1):
+            def hop(h=h):
+                for d in range(2):
+                    if h <= HOPS[d]:
+                        fc(d, h - 1, t - h).wait_recv()
+                        if h < HOPS[d]:
+                            fc(d, h, t - h).start()
+
+            when((t - h >= 0) & (t - h < NB), hop)
+
+    def compute(b):
+        rows = pl.ds(pl.multiple_of(b * BR, BR), BR)
+        lhs = jnp.concatenate([fg[s, rows, :] for s in range(NZ)], axis=1)
+        for d in (2, 1, 3, 0):
+            acc = jnp.dot(
+                lhs, wg[(y + d) % NY].reshape(NZ * KD, COLS), preferred_element_type=jnp.float32
+            )
+            if d == 0:
+                o_ref[rows, :] = acc
+            else:
+                ys[d - 1, rows, :] = acc.astype(jnp.bfloat16)
+                yc(d, b).start()
+
+    def finish(b):
+        rows = pl.ds(pl.multiple_of(b * BR, BR), BR)
+        total = o_ref[rows, :]
+        for d in (1, 3, 2):
+            yc(d, b).wait_recv()
+            total = total + yr[d - 1, rows, :].astype(jnp.float32)
+        o_ref[rows, :] = total
+
+    forward(1, True)
+    from_x(0)
+    from_x(1)
+    forward(2, True)
+    from_x(2)
+    wc(1, 0, c).start()
+    wc(2, 0, c).start()
+    from_relay(0)
+    from_relay(1)
+    forward(3, True)
+    from_x(3)
+    from_x(4)
+    wc(1, 1, c).start()
+    wc(2, 1, c).start()
+    from_relay(2)
+    from_relay(3)
+    wc(3, 0, c).start()
+    from_relay(4)
+    wc(3, 1, c).start()
+    for h in range(2):
+        for i in range(4):
+            wc(i, h, 1 - c).wait_recv()
+
+    def tick(t, carry):
+        forward(t, False)
+        compute(t - 4)
+
+        @pl.when(t > 4)
+        def _():
+            finish(t - 5)
+
+        return carry
+
+    lax.fori_loop(4, NB + 4, tick, 0)
+    finish(NB - 1)
+
+    for k in range(1, NZ):
+        wz(k).wait_send()
+    for d in range(2):
+        for g in range(len(GROUPS)):
+            wx(d, g, x).wait_send()
+            wr(d, g, x).wait_send()
+    for i in range(4):
+        for h in range(2):
+            wc(i, h, c).wait_send()
+
+    def drain(b, carry):
+        for d in range(2):
+            for h in range(HOPS[d]):
+                fc(d, h, b).wait_send()
+        for d in range(1, NY):
+            yc(d, b).wait_send()
+        return carry
+
+    lax.fori_loop(0, NB, drain, 0)
+
+
+def base_product(features, projection_weight):
+    dma = pltpu.SemaphoreType.DMA
+    return pl.pallas_call(
+        base_kernel,
+        out_shape=jax.ShapeDtypeStruct((ROWS, COLS), jnp.float32),
+        in_specs=[pl.BlockSpec(memory_space=pl.ANY)] * 2,
+        out_specs=pl.BlockSpec(memory_space=pltpu.VMEM),
+        scratch_shapes=[
+            pltpu.VMEM((NZ, ROWS, KD), jnp.bfloat16),
+            pltpu.VMEM((NX, NZ, KD, COLS), jnp.bfloat16),
+            pltpu.VMEM((NY - 1, ROWS, COLS), jnp.bfloat16),
+            pltpu.VMEM((NY - 1, ROWS, COLS), jnp.bfloat16),
+            dma((2,)),
+            dma((NZ - 1,)), dma((NZ - 1,)),
+            dma((2, len(GROUPS))), dma((2, len(GROUPS))),
+            dma((2, len(GROUPS))), dma((2, len(GROUPS))),
+            dma((4, 2)), dma((4, 2)),
+            dma((2, 4, NB)), dma((2, 4, NB)),
+            dma((NY - 1, NB)), dma((NY - 1, NB)),
+        ],
+        compiler_params=pltpu.CompilerParams(
+            collective_id=0, has_side_effects=True, vmem_limit_bytes=40 * 1024 * 1024
+        ),
+        cost_estimate=pl.CostEstimate(
+            flops=2 * ROWS * NZ * KD * NY * COLS, bytes_accessed=16 * 1024 * 1024, transcendentals=0
+        ),
+    )(features, projection_weight)
 
 
 def on_device(features, token_adapter_index, projection_weight, shrink_weight, expand_weight):
@@ -22,18 +276,7 @@
         rows, rank_column_values
     )
     lowrank_delta = jnp.dot(widened_rank, expand_weight, preferred_element_type=jnp.float32)
-    base_partial_output = lax.psum_scatter(
-        lax.dot_general(
-            projection_weight,
-            features,
-            (((0,), (1,)), ((), ())),
-            preferred_element_type=jnp.float32,
-        ),
-        "tensor",
-        scatter_dimension=0,
-        tiled=True,
-    ).T
-    return base_partial_output + lowrank_delta
+    return base_product(features, projection_weight) + lowrank_delta
 
 
 def solution(mesh):

time: 307 us -> 221 us (0.72)
  waiting for transfers between devices: 113 us -> 0 us
  Pallas kernels: 0 us -> 60.5 us
  matrix products: 21.5 us -> 5.55 us
  between operations: 13.4 us -> 0.06 us
    reduce_scatter x1 -> x0, waiting for transfers between devices: 113 us -> none  [on_device(): lax.psum_scatter(lax.dot_general(projection_weight, features, (((0,), (1,...]
    pallas_call x0 -> x1, Pallas kernels: none -> 60.5 us  [base_product(): pl.pallas_call(base_kernel, out_shape=jax.ShapeDtypeStruct((ROWS, COLS),...]
    dot_general x1 -> x0, matrix products: 14.3 us -> none  [on_device(): lax.dot_general(projection_weight, features, (((0,), (1,)), ((), ())), pr...]
    psum x1, blocking collectives: 151 us -> 148 us  [on_device(): shrink = lax.psum(partial_shrink, 'tensor')]
  transfers between devices with their start and end apart: 1 -> 0, of which waited for: 1 -> 0; matrix products, arithmetic and copies ran while one was open for 2% -> 0% of each run, Pallas kernels for 0% -> 0%
where the time goes in v1:
time: 221 us; the launch traced here: 220 us
  blocking collectives  148 us (67%)
  Pallas kernels  60.5 us (27%)
  matrix products  5.55 us (3%)
  other arithmetic  3.54 us (2%)
  local copies, waits for them, and re-layouts  2.48 us (1%)
    psum x1, blocking collectives, on_device(): shrink = lax.psum(partial_shrink, 'tensor')  148 us
    pallas_call x1, Pallas kernels, base_product(): pl.pallas_call(base_kernel, out_shape=jax.ShapeDtypeStruct((ROWS, COLS),...  60.5 us

profile of v1, /device:TPU:4, one launch (start us, length us, event | category | flops | bytes accessed | tf_op | source)
XLA Modules:
  0.0 219.8 jit_solution(12367780266711818361)
XLA Ops:
  0.0 0.0 copy-start
  0.0 0.9 fusion
  0.9 0.7 copy-done
  1.6 2.8 %fusion.1 = f32[768,4096]{0,1:T(8,128)S(1)} fusion(bf16[768,256]{1,0:T(8,128)(2,1)} %f_ref.1, bf16[256,4096]{1,0:T(8,128)(2,1)S(1)} %copy-done), kind=kOutput, calls=%fused_computation.5 | convolution fusion | flops 1610612736 | bytes 15073280 | tf_op jit(solution)/shard_map/dot_general | solution.py:269
  4.5 2.3 %select_reduce_fusion = f32[768,64]{0,1:T(8,128)S(1)} fusion(f32[768,64,64]{0,2,1:T(8,128)S(1)} %bitcast.6, pred[768,64]{0,1:T(8,128)(4,1)S(1)} %get-tuple-element.6), kind=kLoop, calls=%fused_computation | loop fusion | flops 6242304 | bytes 12828672 | tf_op jit(solution)/shard_map/reduce_sum | solution.py:272
  6.7 0.0 copy-start.1
  6.7 147.6 %all-reduce.1 = bf16[768,64]{0,1:T(8,128)(2,1)S(1)} all-reduce(f32[768,64]{0,1:T(8,128)S(1)} %select_reduce_fusion), channel_id=1, replica_groups=mesh['dp'=8,'tensor'=32] {'tensor'}, use_global_device_ids=true, to_apply=%region_1.2 | all-reduce | flops 49152 | bytes 294912 | tf_op jit(solution)/shard_map/psum | solution.py:273
  154.3 0.0 copy-start.2
  154.3 0.4 broadcast_multiply_fusion
  154.7 0.0 copy-start.3
  154.8 0.0 copy-done.1
  154.8 1.7 copy-done.2
  156.5 60.5 %shard_map.55 = f32[768,256]{1,0:T(8,128)S(1)} custom-call(bf16[768,256]{1,0:T(8,128)(2,1)S(1)} %copy-done.1, bf16[256,8192]{1,0:T(8,128)(2,1)S(1)} %copy-done.2), custom_call_target="tpu_custom_call" | custom-call | flops 3221225472 | bytes 16777216 | tf_op jit(solution)/shard_map/pallas_call | solution.py:236
  217.1 0.0 copy-done.3
  217.1 2.7 %convolution_add_fusion = f32[768,256]{1,0:T(8,128)} fusion(f32[768,256]{1,0:T(8,128)S(1)} %shard_map.55, bf16[768,4096]{0,1:T(8,128)(2,1)S(1)} %bitcast.7, bf16[4096,256]{1,0:T(8,128)(2,1)S(1)} %copy-done.3), kind=kOutput, calls=%fused_computation.2 | convolution fusion | flops 1610809344 | bytes 9961472 | tf_op jit(solution)/shard_map/dot_general | solution.py:278
Async XLA Ops:
  0.0 1.6 copy-start
  6.7 148.0 %copy-start.1 = (bf16[768,256]{1,0:T(8,128)(2,1)S(1)}, bf16[768,256]{1,0:T(8,128)(2,1)}, u32[]{:S(2)}) copy-start(bf16[768,256]{1,0:T(8,128)(2,1)} %f_ref.1) | copy-start | bytes 1179652
  154.3 2.2 copy-start.2
  154.7 62.3 %copy-start.3 = (bf16[4096,256]{1,0:T(8,128)(2,1)S(1)}, bf16[4096,256]{1,0:T(8,128)(2,1)}, u32[]{:S(2)}) copy-start(bf16[4096,256]{1,0:T(8,128)(2,1)} %param.9) | copy-start | bytes 6291460

commit v2 on v1

v2 whole, which is shorter than its diff:
```python
import jax
import jax.numpy as jnp
from jax import lax
from jax.experimental import pallas as pl
from jax.experimental.pallas import tpu as pltpu
from jax.sharding import PartitionSpec as P

ADAPTER_RANK = 64
NX, NC, NY, NZ = 4, 2, 4, 8
ROWS, KD, COLS = 768, 256, 256
RANKS = 4096
PACKED = ROWS // 2
PY = PACKED // NY
PZ = 16
ZS = PY // PZ
CHUNKS = ((0, 128), (128, 128), (256, 128), (384, 128), (512, 128), (640, 128))
NB = len(CHUNKS)


def hops(d, b):
    return 3 + (b + d) % 2


KORD = (0, 1, 7, 2, 6, 3, 5, 4)
SLOT = {k: s for s, k in enumerate(KORD)}
GROUPS = ((0, 1), (1, 2), (3, 2), (5, 2), (7, 1))
GROUP_OF = {KORD[s]: g for g, (s0, n) in enumerate(GROUPS) for s in range(s0, s0 + n)}
HALF = KD // NC
QUART = HALF // 2
def kernel(
    f_ref, i_ref, w_ref, s_ref, e_ref, o_ref,
    fg, wg, ys, yr, sv, ev, idx, acc128, packed, fromy, part, fromz, shb, shr,
    loc, wzs, wzr, wxs, wxr, wrs, wrr, wcs, wcr, fs, fr, yss, yrs,
    ls, lr,
):
    dp, tensor = lax.axis_index("dp"), lax.axis_index("tensor")
    x, c = dp // NC, dp % NC
    y, z = tensor // NZ, tensor % NZ

    def at_z(k):
        return {"tensor": y * NZ + (z + k) % NZ}

    def at_y(d):
        return {"tensor": ((y + d) % NY) * NZ + z}

    def at_x(d):
        return {"dp": ((x + d) % NX) * NC + c}

    sibling = {"dp": x * NC + (1 - c)}

    own_f = pltpu.make_async_copy(f_ref, fg.at[0], loc.at[0])
    own_f.start()

    def w_part(zz):
        return w_ref.at[
            pl.ds(pl.multiple_of(c * HALF, HALF), HALF),
            pl.ds(pl.multiple_of((x * NZ + zz) * COLS, COLS), COLS),
        ]

    half = pl.ds(pl.multiple_of(c * HALF, HALF), HALF)
    own_w = pltpu.make_async_copy(w_part(z), wg.at[x, 0, half], loc.at[1])
    own_w.start()

    own_s = pltpu.make_async_copy(s_ref, sv, loc.at[2])
    own_s.start()
    own_e = pltpu.make_async_copy(e_ref, ev, loc.at[3])
    own_e.start()

    peers = (
        [at_z(k) for k in range(1, NZ)]
        + [at_y(d) for d in range(1, NY)]
        + [at_x(1), at_x(-1 + NX), sibling]
    )
    barrier = pltpu.get_barrier_semaphore()
    for peer in peers:
        pl.semaphore_signal(barrier, inc=1, device_id=peer, device_id_type=pl.DeviceIdType.MESH)
    pl.semaphore_wait(barrier, len(peers))

    def remote(src, dst, s, r, dev):
        return pltpu.make_async_remote_copy(
            src_ref=src, dst_ref=dst, send_sem=s, recv_sem=r,
            device_id=dev, device_id_type=pl.DeviceIdType.MESH,
        )

    def wz(k):
        return remote(
            w_part((z + k) % NZ), wg.at[x, SLOT[k], half], wzs.at[0], wzr.at[GROUP_OF[k]], at_z(k)
        )

    def wx(d, g, owner):
        s0, n = GROUPS[g]
        part = wg.at[owner, pl.ds(s0, n), half]
        return remote(part, part, wxs.at[0], wxr.at[d, g], at_x(1 if d == 0 else NX - 1))

    def wr(d, g, owner):
        s0, n = GROUPS[g]
        rows = pl.ds(pl.multiple_of(c * HALF + d * QUART, QUART), QUART)
        part = wg.at[owner, pl.ds(s0, n), rows]
        return remote(part, part, wrs.at[0], wrr.at[g], at_x(1 if d == 0 else NX - 1))

    def wc(i, h, which):
        owner = (x + (0, NX - 1, 1, 2)[i]) % NX
        part = wg.at[owner, pl.ds(4 * h, 4), pl.ds(pl.multiple_of(which * HALF, HALF), HALF)]
        return remote(part, part, wcs.at[0], wcr.at[0], sibling)

    def rows_of(b):
        return pl.ds(*CHUNKS[b])

    def fc(d, h, b):
        src = SLOT[h] if d == 0 else SLOT[(NZ - h) % NZ]
        dst = SLOT[h + 1] if d == 0 else SLOT[NZ - 1 - h]
        rows = rows_of(b)
        return remote(
            fg.at[src, rows], fg.at[dst, rows], fs.at[0], fr.at[d, h, b], at_z(1 if d == 0 else NZ - 1)
        )

    def yc(d, b):
        rows = rows_of(b)
        return remote(ys.at[d - 1, rows], yr.at[d - 1, rows], yss.at[0], yrs.at[b], at_y(d))

    def sent(ref, sem):
        remote(ref, ref, sem, sem, sibling).wait_send()

    def received(ref, sem):
        remote(ref, ref, sem, sem, sibling).wait_recv()

    def l1(d):
        rows = pl.ds(pl.multiple_of(((y + d) % NY) * PY, PY), PY)
        return remote(packed.at[rows], fromy.at[d - 1], ls.at[0], lr.at[0], at_y(d))

    def l2(k):
        rows = pl.ds(pl.multiple_of(((z + k) % NZ) * PZ, PZ), PZ)
        return remote(part.at[rows], fromz.at[k - 1], ls.at[1], lr.at[1], at_z(k))

    def l3(k, source):
        piece = shb.at[pl.ds(pl.multiple_of(y * PY + source * PZ, PZ), PZ)]
        return remote(piece, piece, ls.at[2], lr.at[2], at_z(k))

    def l4(d, source):
        piece = shb.at[pl.ds(pl.multiple_of(source * PY, PY), PY)]
        return remote(piece, piece, ls.at[3], lr.at[3], at_y(d))

    def adapters_of_tokens():
        eye = lax.broadcasted_iota(jnp.int32, (128, 128), 0) == lax.broadcasted_iota(
            jnp.int32, (128, 128), 1
        )
        upper = (lax.broadcasted_iota(jnp.int32, (128, 128), 1) >= ADAPTER_RANK).astype(jnp.float32)
        ones = jnp.ones((128, 128), jnp.bfloat16)
        for i in range(ROWS // 128):
            row = jnp.broadcast_to(i_ref[pl.ds(i, 1), :].astype(jnp.float32), (128, 128))
            diagonal = jnp.where(eye, row, 0.0).astype(jnp.bfloat16)
            spread = jnp.dot(diagonal, ones, preferred_element_type=jnp.float32)
            idx[pl.ds(i * 128, 128), :] = spread - upper
        acc128[...] = jnp.zeros_like(acc128)

    def shrink_columns(j, carry):
        columns = sv[:, pl.ds(pl.multiple_of(j * 256, 256), 256)]
        first = (4 * j).astype(jnp.float32)
        for r in range(3):
            rows = pl.ds(r * 256, 256)
            out = jnp.dot(fg[0, rows, :], columns, preferred_element_type=jnp.float32)
            which = idx[rows, :]
            acc128[rows, :] += jnp.where(which == first, out[:, :128], 0.0) + jnp.where(
                which == first + 2.0, out[:, 128:], 0.0
            )
        return carry

    def shrink_part(i):
        lax.fori_loop(4 * i, 4 * i + 4, shrink_columns, 0)

    lower = lax.broadcasted_iota(jnp.int32, (96, 128), 1) < ADAPTER_RANK

    def shrink_to_y():
        for r in range(PACKED // 96):
            a = acc128[pl.ds(r * 96, 96), :]
            b = acc128[pl.ds(PACKED + r * 96, 96), :]
            packed[pl.ds(r * 96, 96), :] = jnp.where(
                lower, a + pltpu.roll(a, ADAPTER_RANK, 1), b + pltpu.roll(b, ADAPTER_RANK, 1)
            )
        for d in (2, 1, 3):
            l1(d).start()

    def shrink_to_z():
        received(fromy, lr.at[0])
        part[...] = (
            packed[pl.ds(pl.multiple_of(y * PY, PY), PY), :] + fromy[0] + fromy[1] + fromy[2]
        )
        for k in range(1, NZ):
            @pl.when((z + k) % NZ < ZS)
            def _(k=k):
                l2(k).start()

    def shrunk_to_z():
        @pl.when(z < ZS)
        def _():
            total = part[pl.ds(pl.multiple_of(z * PZ, PZ), PZ), :]
            received(fromz, lr.at[1])
            for k in range(1, NZ):
                total = total + fromz[k - 1]
            shb[pl.ds(pl.multiple_of(y * PY + z * PZ, PZ), PZ), :] = total.astype(jnp.bfloat16)
            for k in range(1, NZ):
                l3(k, z).start()

    def shrunk_to_y():
        @pl.when(z < ZS)
        def _():
            received(shb.at[pl.ds(0, (ZS - 1) * PZ)], lr.at[2])

        @pl.when(z >= ZS)
        def _():
            received(shb.at[pl.ds(0, ZS * PZ)], lr.at[2])

        for d in (2, 1, 3):
            l4(d, y).start()

    def shrunk_here():
        received(shb.at[pl.ds(0, (NY - 1) * PY)], lr.at[3])
        for r in range(PACKED // 96):
            a = shb[pl.ds(r * 96, 96), :].astype(jnp.float32)
            b = pltpu.roll(a, ADAPTER_RANK, 1)
            shr[pl.ds(r * 96, 96), :] = jnp.where(lower, a, b)
            shr[pl.ds(PACKED + r * 96, 96), :] = jnp.where(lower, b, a)

    def expand(b):
        rows, n = rows_of(b), CHUNKS[b][1]
        which, values = idx[rows, :], shr[rows, :]

        def step(j, total):
            first = (8 * j).astype(jnp.float32)
            wide = jnp.concatenate(
                [jnp.where(which == first + 2.0 * i, values, 0.0).astype(jnp.bfloat16) for i in range(4)],
                axis=1,
            )
            return total + jnp.dot(
                wide, ev[pl.ds(pl.multiple_of(j * 512, 512), 512), :], preferred_element_type=jnp.float32
            )

        o_ref[rows, :] += lax.fori_loop(0, RANKS // 512, step, jnp.zeros((n, COLS), jnp.float32))

    left, right = (x + NX - 1) % NX, (x + 1) % NX

    def from_x(g):
        wx(0, g, left).wait_recv()
        wr(0, g, left).start()
        wx(1, g, right).wait_recv()
        wr(1, g, right).start()

    def from_relay(g):
        s0, n = GROUPS[g]
        received(wg.at[(x + 2) % NX, pl.ds(s0, n), half], wrr.at[g])

    def own(b):
        for d in range(2):
            fc(d, 0, b).start()

    def pass_on(h, b):
        for d in range(2):
            if h <= hops(d, b):
                fc(d, h - 1, b).wait_recv()
            if h < hops(d, b):
                fc(d, h, b).start()

    def from_z(g):
        s0, n = GROUPS[g]
        received(wg.at[x, pl.ds(s0, n), half], wzr.at[g])
        wx(0, g, x).start()
        wx(1, g, x).start()

    def weight_to_z():
        for k in KORD[1:]:
            wz(k).start()
        own_w.wait()
        wx(0, 0, x).start()
        wx(1, 0, x).start()

    def shrink_start():
        adapters_of_tokens()
        own_s.wait()

    def weights_here():
        other = pl.ds(pl.multiple_of((1 - c) * HALF, HALF), HALF)
        received(wg.at[pl.ds(0, NX), pl.ds(0, NZ), other], wcr.at[0])

    def expand_here():
        own_e.wait()
        shrunk_here()

    def product(b):
        rows = rows_of(b)
        lhs = jnp.concatenate([fg[s, rows, :] for s in range(NZ)], axis=1)
        for d in (2, 1, 3, 0):
            acc = jnp.dot(
                lhs, wg[(y + d) % NY].reshape(NZ * KD, COLS), preferred_element_type=jnp.float32
            )
            if d == 0:
                o_ref[rows, :] = acc
            else:
                ys[d - 1, rows, :] = acc.astype(jnp.bfloat16)
                yc(d, b).start()

    def finish(b):
        rows = rows_of(b)
        received(yr.at[pl.ds(0, NY - 1), rows], yrs.at[b])
        total = o_ref[rows, :]
        for d in (1, 3, 2):
            total = total + yr[d - 1, rows, :].astype(jnp.float32)
        o_ref[rows, :] = total

    own_f.wait()
    weight_to_z()
    own(0)
    own(1)
    shrink_start()
    shrink_part(0)
    shrink_part(1)
    shrink_part(2)
    shrink_part(3)
    shrink_to_y()
    from_z(1)
    from_x(0)
    pass_on(1, 0)
    pass_on(1, 1)
    own(2)
    own(3)
    from_z(2)
    wc(0, 0, c).start()
    from_x(1)
    shrink_to_z()
    pass_on(2, 0)
    pass_on(2, 1)
    pass_on(1, 2)
    pass_on(1, 3)
    from_z(3)
    from_relay(0)
    from_x(2)
    shrunk_to_z()
    from_z(4)
    wc(0, 1, c).start()
    pass_on(3, 0)
    pass_on(3, 1)
    own(4)
    own(5)
    from_relay(1)
    wc(1, 0, c).start()
    wc(2, 0, c).start()
    from_x(3)
    from_x(4)
    shrunk_to_y()
    pass_on(2, 2)
    pass_on(2, 3)
    wc(1, 1, c).start()
    wc(2, 1, c).start()
    from_relay(2)
    from_relay(3)
    wc(3, 0, c).start()
    pass_on(1, 4)
    pass_on(1, 5)
    from_relay(4)
    wc(3, 1, c).start()
    weights_here()
    pass_on(4, 0)
    pass_on(4, 1)
    product(0)
    product(1)
    pass_on(3, 2)
    pass_on(3, 3)
    expand_here()
    pass_on(2, 4)
    pass_on(2, 5)
    expand(0)
    pass_on(4, 2)
    product(2)
    pass_on(4, 3)
    product(3)
    pass_on(3, 4)
    pass_on(3, 5)
    expand(1)
    pass_on(4, 4)
    product(4)
    pass_on(4, 5)
    product(5)
    expand(2)
    expand(3)
    expand(4)
    expand(5)
    finish(0)
    finish(1)
    finish(2)
    finish(3)
    finish(4)
    finish(5)

    sent(wg.at[0, pl.ds(0, NZ - 1), pl.ds(0, HALF)], wzs.at[0])
    sent(wg.at[pl.ds(0, 2), pl.ds(0, NZ), pl.ds(0, HALF)], wxs.at[0])
    sent(wg.at[0, pl.ds(0, NZ), pl.ds(0, HALF)], wrs.at[0])
    sent(wg.at[pl.ds(0, NX), pl.ds(0, NZ), pl.ds(0, HALF)], wcs.at[0])
    sent(fg.at[pl.ds(0, NZ - 1)], fs.at[0])
    sent(ys, yss.at[0])
    sent(fromy, ls.at[0])

    @pl.when(z < ZS)
    def _():
        sent(part.at[pl.ds(0, (ZS - 1) * PZ)], ls.at[1])
        sent(shb.at[pl.ds(0, (NZ - 1) * PZ)], ls.at[2])

    @pl.when(z >= ZS)
    def _():
        sent(part.at[pl.ds(0, ZS * PZ)], ls.at[1])

    sent(shb.at[pl.ds(0, (NY - 1) * PY)], ls.at[3])


def on_device(features, token_adapter_index, projection_weight, shrink_weight, expand_weight):
    dma = pltpu.SemaphoreType.DMA
    anywhere = pl.BlockSpec(memory_space=pltpu.HBM)
    vmem = pl.BlockSpec(memory_space=pltpu.VMEM)
    return pl.pallas_call(
        kernel,
        out_shape=jax.ShapeDtypeStruct((ROWS, COLS), jnp.float32),
        in_specs=[anywhere, vmem, anywhere, anywhere, anywhere],
        out_specs=vmem,
        scratch_shapes=[
            pltpu.VMEM((NZ, ROWS, KD), jnp.bfloat16),
            pltpu.VMEM((NX, NZ, KD, COLS), jnp.bfloat16),
            pltpu.VMEM((NY - 1, ROWS, COLS), jnp.bfloat16),
            pltpu.VMEM((NY - 1, ROWS, COLS), jnp.bfloat16),
            pltpu.VMEM((KD, RANKS), jnp.bfloat16),
            pltpu.VMEM((RANKS, COLS), jnp.bfloat16),
            pltpu.VMEM((ROWS, 128), jnp.float32),
            pltpu.VMEM((ROWS, 128), jnp.float32),
            pltpu.VMEM((PACKED, 128), jnp.float32),
            pltpu.VMEM((NY - 1, PY, 128), jnp.float32),
            pltpu.VMEM((PY, 128), jnp.float32),
            pltpu.VMEM((NZ - 1, PZ, 128), jnp.float32),
            pltpu.VMEM((PACKED, 128), jnp.bfloat16),
            pltpu.VMEM((ROWS, 128), jnp.float32),
            dma((4,)),
            dma((1,)), dma((len(GROUPS),)),
            dma((1,)), dma((2, len(GROUPS))),
            dma((1,)), dma((len(GROUPS),)),
            dma((1,)), dma((1,)),
            dma((1,)), dma((2, 4, NB)),
            dma((1,)), dma((NB,)),
            dma((4,)), dma((4,)),
        ],
        compiler_params=pltpu.CompilerParams(
            collective_id=0, has_side_effects=True, vmem_limit_bytes=62 * 1024 * 1024
        ),
        cost_estimate=pl.CostEstimate(
            flops=2 * ROWS * (NZ * KD * NY * COLS + 2 * KD * RANKS),
            bytes_accessed=16 * 1024 * 1024,
            transcendentals=0,
        ),
    )(
        features,
        token_adapter_index.reshape(ROWS // 128, 128),
        projection_weight,
        shrink_weight,
        expand_weight,
    )


def solution(mesh):
    in_specs = (P("dp", "tensor"), P("dp"), P("tensor", None), P("tensor", None), P(None, "tensor"))
    out_specs = P("dp", "tensor")
    return jax.shard_map(
        on_device, mesh=mesh, in_specs=in_specs, out_specs=out_specs, check_vma=False
    )
```

time: 221 us -> 72.8 us (0.33)
  the two profiles are of different devices: /device:TPU:4 before, /device:TPU:1 now
where the time goes in v2:
time: 72.8 us; the launch traced here: 72.6 us
  Pallas kernels  70.6 us (97%)
  local copies, waits for them, and re-layouts  2.06 us (3%)
    pallas_call x1, Pallas kernels, on_device(): pl.pallas_call(kernel, out_shape=jax.ShapeDtypeStruct((ROWS, COLS), jnp.f...  70.6 us
    unnamed x1, local copies, waits for them, and re-layouts  2.06 us

profile of v2, /device:TPU:1, one launch (start us, length us, event | category | flops | bytes accessed | tf_op | source)
XLA Modules:
  0.0 72.6 jit_solution(6859919240657139693)
XLA Ops:
  0.0 70.6 %shard_map.55 = f32[768,256]{1,0:T(8,128)} custom-call(bf16[768,256]{1,0:T(8,128)(2,1)} %f_ref.1, s32[6,128]{1,0:T(8,128)} %bitcast.1, bf16[256,8192]{1,0:T(8,128)(2,1)} %w_ref.1, bf16[256,4096]{1,0:T(8,128)(2,1)} %s_ref.1, bf16[4096,256]{1,0:T(8,128)(2,1)} %e_ref.1), custom_call_target="tpu_custom_call" | custom-call | flops 6442450944 | bytes 16777216 | tf_op jit(solution)/shard_map/pallas_call | solution.py:417
  70.6 2.1 %copy.7 = f32[768,256]{1,0:T(8,128)} copy(f32[768,256]{1,0:T(8,128)} %shard_map.55) | data formatting | bytes 1572864

commit v3 on v2

--- a/solution.py
+++ b/solution.py
@@ -29,7 +29,7 @@
 QUART = HALF // 2
 def kernel(
     f_ref, i_ref, w_ref, s_ref, e_ref, o_ref,
-    fg, wg, ys, yr, sv, ev, idx, acc128, packed, fromy, part, fromz, shb, shr,
+    fg, wg, ys, yr, sv, ev, idx, acc, acc128, packed, fromy, part, fromz, shb, shr,
     loc, wzs, wzr, wxs, wxr, wrs, wrr, wcs, wcr, fs, fr, yss, yrs,
     ls, lr,
 ):
@@ -221,8 +221,9 @@
             shr[pl.ds(r * 96, 96), :] = jnp.where(lower, a, b)
             shr[pl.ds(PACKED + r * 96, 96), :] = jnp.where(lower, b, a)
 
-    def expand(b):
-        rows, n = rows_of(b), CHUNKS[b][1]
+    def expand(i, j):
+        n = sum(n for _, n in CHUNKS[i : j + 1])
+        rows = pl.ds(CHUNKS[i][0], n)
         which, values = idx[rows, :], shr[rows, :]
 
         def step(j, total):
@@ -285,17 +286,24 @@
         own_e.wait()
         shrunk_here()
 
+    def product_start(i, j):
+        rows = pl.ds(CHUNKS[i][0], sum(n for _, n in CHUNKS[i : j + 1]))
+        lhs = jnp.concatenate([fg[s, rows, :] for s in range(NZ - 1)], axis=1)
+        for d in range(NY):
+            weights = wg[(y + d) % NY, pl.ds(0, NZ - 1)].reshape((NZ - 1) * KD, COLS)
+            acc[d, rows, :] = jnp.dot(lhs, weights, preferred_element_type=jnp.float32)
+
     def product(b):
         rows = rows_of(b)
-        lhs = jnp.concatenate([fg[s, rows, :] for s in range(NZ)], axis=1)
+        lhs = fg[NZ - 1, rows, :]
         for d in (2, 1, 3, 0):
-            acc = jnp.dot(
-                lhs, wg[(y + d) % NY].reshape(NZ * KD, COLS), preferred_element_type=jnp.float32
+            out = acc[d, rows, :] + jnp.dot(
+                lhs, wg[(y + d) % NY, NZ - 1], preferred_element_type=jnp.float32
             )
             if d == 0:
-                o_ref[rows, :] = acc
+                o_ref[rows, :] = out
             else:
-                ys[d - 1, rows, :] = acc.astype(jnp.bfloat16)
+                ys[d - 1, rows, :] = out.astype(jnp.bfloat16)
                 yc(d, b).start()
 
     def finish(b):
@@ -313,76 +321,76 @@
     shrink_start()
     shrink_part(0)
     shrink_part(1)
+    from_x(0)
+    from_z(1)
     shrink_part(2)
     shrink_part(3)
     shrink_to_y()
-    from_z(1)
-    from_x(0)
+    from_z(2)
+    wc(0, 0, c).start()
+    from_x(1)
+    from_relay(0)
+    from_z(3)
+    shrink_to_z()
+    from_x(2)
+    from_relay(1)
+    from_z(4)
+    wc(0, 1, c).start()
+    wc(1, 0, c).start()
+    wc(2, 0, c).start()
     pass_on(1, 0)
     pass_on(1, 1)
     own(2)
     own(3)
-    from_z(2)
-    wc(0, 0, c).start()
-    from_x(1)
-    shrink_to_z()
+    from_x(3)
+    from_relay(2)
+    wc(3, 0, c).start()
+    shrunk_to_z()
+    from_x(4)
+    wc(1, 1, c).start()
+    wc(2, 1, c).start()
     pass_on(2, 0)
     pass_on(2, 1)
+    from_relay(3)
+    from_relay(4)
+    wc(3, 1, c).start()
+    shrunk_to_y()
     pass_on(1, 2)
     pass_on(1, 3)
-    from_z(3)
-    from_relay(0)
-    from_x(2)
-    shrunk_to_z()
-    from_z(4)
-    wc(0, 1, c).start()
     pass_on(3, 0)
     pass_on(3, 1)
     own(4)
     own(5)
-    from_relay(1)
-    wc(1, 0, c).start()
-    wc(2, 0, c).start()
-    from_x(3)
-    from_x(4)
-    shrunk_to_y()
     pass_on(2, 2)
     pass_on(2, 3)
-    wc(1, 1, c).start()
-    wc(2, 1, c).start()
-    from_relay(2)
-    from_relay(3)
-    wc(3, 0, c).start()
+    expand_here()
     pass_on(1, 4)
     pass_on(1, 5)
-    from_relay(4)
-    wc(3, 1, c).start()
     weights_here()
+    product_start(0, 1)
     pass_on(4, 0)
     pass_on(4, 1)
     product(0)
     product(1)
     pass_on(3, 2)
     pass_on(3, 3)
-    expand_here()
     pass_on(2, 4)
     pass_on(2, 5)
-    expand(0)
+    product_start(2, 3)
     pass_on(4, 2)
     product(2)
     pass_on(4, 3)
     product(3)
     pass_on(3, 4)
     pass_on(3, 5)
-    expand(1)
+    product_start(4, 5)
+    expand(0, 1)
     pass_on(4, 4)
     product(4)
     pass_on(4, 5)
     product(5)
-    expand(2)
-    expand(3)
-    expand(4)
-    expand(5)
+    expand(2, 3)
+    expand(4, 5)
     finish(0)
     finish(1)
     finish(2)
@@ -427,6 +435,7 @@
             pltpu.VMEM((KD, RANKS), jnp.bfloat16),
             pltpu.VMEM((RANKS, COLS), jnp.bfloat16),
             pltpu.VMEM((ROWS, 128), jnp.float32),
+            pltpu.VMEM((NY, ROWS, COLS), jnp.float32),
             pltpu.VMEM((ROWS, 128), jnp.float32),
             pltpu.VMEM((PACKED, 128), jnp.float32),
             pltpu.VMEM((NY - 1, PY, 128), jnp.float32),
@@ -444,7 +453,7 @@
             dma((4,)), dma((4,)),
         ],
         compiler_params=pltpu.CompilerParams(
-            collective_id=0, has_side_effects=True, vmem_limit_bytes=62 * 1024 * 1024
+            collective_id=0, has_side_effects=True, vmem_limit_bytes=52 * 1024 * 1024
         ),
         cost_estimate=pl.CostEstimate(
             flops=2 * ROWS * (NZ * KD * NY * COLS + 2 * KD * RANKS),

time: 72.8 us -> 66.5 us (0.913)
  the two profiles are of different devices: /device:TPU:1 before, /device:TPU:4 now
where the time goes in v3:
time: 66.5 us; the launch traced here: 66.2 us
  Pallas kernels  63.6 us (96%)
  local copies, waits for them, and re-layouts  2.56 us (4%)
    pallas_call x1, Pallas kernels, on_device(): pl.pallas_call(kernel, out_shape=jax.ShapeDtypeStruct((ROWS, COLS), jnp.f...  63.6 us
    unnamed x5, local copies, waits for them, and re-layouts  2.56 us

profile of v3, /device:TPU:4, one launch (start us, length us, event | category | flops | bytes accessed | tf_op | source)
XLA Modules:
  0.0 66.2 jit_solution(11657343483078710911)
XLA Ops:
  0.0 0.0 copy-start
  0.0 1.0 %copy-done = bf16[768,256]{1,0:T(8,128)(2,1)S(1)} copy-done((bf16[768,256]{1,0:T(8,128)(2,1)S(1)}, bf16[768,256]{1,0:T(8,128)(2,1)}, u32[]{:S(2)}) %copy-start) | copy-done | bytes 393240
  1.0 0.0 copy-start.1
  1.0 0.7 %copy-done.1 = s32[768]{0:T(1024)S(1)} copy-done((s32[768]{0:T(1024)S(1)}, s32[768]{0:T(1024)}, u32[]{:S(2)}) %copy-start.1) | copy-done | bytes 3096
  1.7 63.6 %shard_map.55 = f32[768,256]{1,0:T(8,128)S(1)} custom-call(bf16[768,256]{1,0:T(8,128)(2,1)S(1)} %copy-done, s32[6,128]{1,0:T(8,128)S(1)} %bitcast.1, bf16[256,8192]{1,0:T(8,128)(2,1)} %w_ref.1, bf16[256,4096]{1,0:T(8,128)(2,1)} %s_ref.1, bf16[4096,256]{1,0:T(8,128)(2,1)} %e_ref.1), custom_call_target="tpu_custom_call" | custom-call | flops 6442450944 | bytes 16777216 | tf_op jit(solution)/shard_map/pallas_call | solution.py:425
  65.3 0.9 %copy.7 = f32[768,256]{1,0:T(8,128)} copy(f32[768,256]{1,0:T(8,128)S(1)} %shard_map.55) | data formatting | bytes 1572864
Async XLA Ops:
  0.0 1.0 %copy-start = (bf16[768,256]{1,0:T(8,128)(2,1)S(1)}, bf16[768,256]{1,0:T(8,128)(2,1)}, u32[]{:S(2)}) copy-start(bf16[768,256]{1,0:T(8,128)(2,1)} %f_ref.1) | copy-start | bytes 1179652
  1.0 0.7 %copy-start.1 = (s32[768]{0:T(1024)S(1)}, s32[768]{0:T(1024)}, u32[]{:S(2)}) copy-start(s32[768]{0:T(1024)} %param.6) | copy-start | bytes 9220

commit v4 on v3

--- a/solution.py
+++ b/solution.py
@@ -48,24 +48,6 @@
 
     sibling = {"dp": x * NC + (1 - c)}
 
-    own_f = pltpu.make_async_copy(f_ref, fg.at[0], loc.at[0])
-    own_f.start()
-
-    def w_part(zz):
-        return w_ref.at[
-            pl.ds(pl.multiple_of(c * HALF, HALF), HALF),
-            pl.ds(pl.multiple_of((x * NZ + zz) * COLS, COLS), COLS),
-        ]
-
-    half = pl.ds(pl.multiple_of(c * HALF, HALF), HALF)
-    own_w = pltpu.make_async_copy(w_part(z), wg.at[x, 0, half], loc.at[1])
-    own_w.start()
-
-    own_s = pltpu.make_async_copy(s_ref, sv, loc.at[2])
-    own_s.start()
-    own_e = pltpu.make_async_copy(e_ref, ev, loc.at[3])
-    own_e.start()
-
     peers = (
         [at_z(k) for k in range(1, NZ)]
         + [at_y(d) for d in range(1, NY)]
@@ -74,6 +56,25 @@
     barrier = pltpu.get_barrier_semaphore()
     for peer in peers:
         pl.semaphore_signal(barrier, inc=1, device_id=peer, device_id_type=pl.DeviceIdType.MESH)
+
+    own_f = pltpu.make_async_copy(f_ref, fg.at[0], loc.at[0])
+    own_f.start()
+
+    def w_part(zz):
+        return w_ref.at[
+            pl.ds(pl.multiple_of(c * HALF, HALF), HALF),
+            pl.ds(pl.multiple_of((x * NZ + zz) * COLS, COLS), COLS),
+        ]
+
+    half = pl.ds(pl.multiple_of(c * HALF, HALF), HALF)
+    own_w = pltpu.make_async_copy(w_part(z), wg.at[x, 0, half], loc.at[1])
+    own_w.start()
+
+    own_s = pltpu.make_async_copy(s_ref, sv, loc.at[2])
+    own_s.start()
+    own_e = pltpu.make_async_copy(e_ref, ev, loc.at[3])
+    own_e.start()
+
     pl.semaphore_wait(barrier, len(peers))
 
     def remote(src, dst, s, r, dev):
@@ -331,7 +332,6 @@
     from_x(1)
     from_relay(0)
     from_z(3)
-    shrink_to_z()
     from_x(2)
     from_relay(1)
     from_z(4)
@@ -345,7 +345,7 @@
     from_x(3)
     from_relay(2)
     wc(3, 0, c).start()
-    shrunk_to_z()
+    shrink_to_z()
     from_x(4)
     wc(1, 1, c).start()
     wc(2, 1, c).start()
@@ -354,24 +354,24 @@
     from_relay(3)
     from_relay(4)
     wc(3, 1, c).start()
-    shrunk_to_y()
     pass_on(1, 2)
     pass_on(1, 3)
+    shrunk_to_z()
     pass_on(3, 0)
     pass_on(3, 1)
     own(4)
     own(5)
+    weights_here()
+    product_start(0, 1)
     pass_on(2, 2)
     pass_on(2, 3)
-    expand_here()
-    pass_on(1, 4)
-    pass_on(1, 5)
-    weights_here()
-    product_start(0, 1)
     pass_on(4, 0)
     pass_on(4, 1)
     product(0)
     product(1)
+    pass_on(1, 4)
+    pass_on(1, 5)
+    shrunk_to_y()
     pass_on(3, 2)
     pass_on(3, 3)
     pass_on(2, 4)
@@ -384,11 +384,12 @@
     pass_on(3, 4)
     pass_on(3, 5)
     product_start(4, 5)
-    expand(0, 1)
     pass_on(4, 4)
     product(4)
     pass_on(4, 5)
     product(5)
+    expand_here()
+    expand(0, 1)
     expand(2, 3)
     expand(4, 5)
     finish(0)

time: 66.5 us -> 66.2 us (level)
  no operation moved by 1% of the time
where the time goes in v4:
time: 66.2 us; the launch traced here: 66 us
  Pallas kernels  63.4 us (96%)
  local copies, waits for them, and re-layouts  2.56 us (4%)
    pallas_call x1, Pallas kernels, on_device(): pl.pallas_call(kernel, out_shape=jax.ShapeDtypeStruct((ROWS, COLS), jnp.f...  63.4 us
    unnamed x5, local copies, waits for them, and re-layouts  2.56 us

profile of v4, /device:TPU:4, one launch (start us, length us, event | category | flops | bytes accessed | tf_op | source)
XLA Modules:
  0.0 66.0 jit_solution(12997211089237724507)
XLA Ops:
  0.0 0.0 copy-start
  0.0 1.0 %copy-done = bf16[768,256]{1,0:T(8,128)(2,1)S(1)} copy-done((bf16[768,256]{1,0:T(8,128)(2,1)S(1)}, bf16[768,256]{1,0:T(8,128)(2,1)}, u32[]{:S(2)}) %copy-start) | copy-done | bytes 393240
  1.0 0.0 copy-start.1
  1.0 0.7 %copy-done.1 = s32[768]{0:T(1024)S(1)} copy-done((s32[768]{0:T(1024)S(1)}, s32[768]{0:T(1024)}, u32[]{:S(2)}) %copy-start.1) | copy-done | bytes 3096
  1.7 63.4 %shard_map.55 = f32[768,256]{1,0:T(8,128)S(1)} custom-call(bf16[768,256]{1,0:T(8,128)(2,1)S(1)} %copy-done, s32[6,128]{1,0:T(8,128)S(1)} %bitcast.1, bf16[256,8192]{1,0:T(8,128)(2,1)} %w_ref.1, bf16[256,4096]{1,0:T(8,128)(2,1)} %s_ref.1, bf16[4096,256]{1,0:T(8,128)(2,1)} %e_ref.1), custom_call_target="tpu_custom_call" | custom-call | flops 6442450944 | bytes 16777216 | tf_op jit(solution)/shard_map/pallas_call | solution.py:426
  65.1 0.9 %copy.7 = f32[768,256]{1,0:T(8,128)} copy(f32[768,256]{1,0:T(8,128)S(1)} %shard_map.55) | data formatting | bytes 1572864
Async XLA Ops:
  0.0 1.0 %copy-start = (bf16[768,256]{1,0:T(8,128)(2,1)S(1)}, bf16[768,256]{1,0:T(8,128)(2,1)}, u32[]{:S(2)}) copy-start(bf16[768,256]{1,0:T(8,128)(2,1)} %f_ref.1) | copy-start | bytes 1179652
  1.0 0.7 %copy-start.1 = (s32[768]{0:T(1024)S(1)}, s32[768]{0:T(1024)}, u32[]{:S(2)}) copy-start(s32[768]{0:T(1024)} %param.6) | copy-start | bytes 9220
